TPU v7x, 256 devices: a whole 4x4x8 slice. The times are simulated.
256 devices in a mesh: front: 64 (over z, y, core), rhs: 4 (over x).
Axes of the slice: x: 4, y: 4, z: 8, core: 2. Of those that a mesh axis runs over, the one named last changes fastest.
Arguments:
- right_side: float32 [32, 4, 8192], P('rhs', None, 'front'), may hold values from -6 to 6
- inverse_top: float32 [8192, 8192], P('front'), as said below
- inverse_second: float32 [8192, 4096], P('front'), as said below
- inverse_third: float32 [8192, 2048], P('front'), as said below
- inverse_fourth: float32 [8192, 1024], P('front'), as said below
- panels: float32 [3, 1024, 8192], P(None, None, 'front'), may hold values from -0.09375 to 0.09375
- targets: int32 [3, 64, 8], P(None, 'front'), may hold values from -1 to 191, as said below
Outputs:
- forward_result: float32 [32, 4, 8192], P('rhs', None, 'front')
- solution: float32 [32, 4, 8192], P('rhs', None, 'front')
Inputs may be any that keep to these rules, and one draw needn't show every extreme that they name: `targets`: for tier k + 1 the devices of one front hold the same list; its live entries are distinct blocks of that front's ancestors in the window (tiers 0 to k, the blocks inside the ancestor's devices), -1 marks an unused slot, each front has 1 to 8 live entries, and on every tier some front has exactly 8. `inverse_top`: within each front of D * 128 rows, with r the row's place in the front, the block is triangular in the elimination order o(r) = (r % 128) * D + r // 128: entry (i, j) is zero when o(j) > o(i); diagonal entries in 1 to 2. `inverse_second`: triangular in the same elimination order within each front, diagonal entries in 1 to 2. `inverse_third`: triangular in the same elimination order within each front, diagonal entries in 1 to 2. `inverse_fourth`: triangular in the same elimination order within each front, diagonal entries in 1 to 2.
All inputs are finite; a program needn't handle non-finite values.
Results may differ from a plain program's by a relative error of at most 0.0001.
Values sent between devices are 32-bit elements; how exact they have to be, the bound alone decides.
A program may use at most 64 MiB of HBM per device.

v0:
```python
import functools

import jax
import jax.numpy as jnp
from jax import lax
from jax.experimental import pallas as pl
from jax.experimental.pallas import tpu as pltpu
from jax.sharding import PartitionSpec as P

F32 = jnp.float32
BF16 = jnp.bfloat16
I32 = jnp.int32
MESH = pl.DeviceIdType.MESH
TIERS = 4
SLOTS = 8
BLOCKS = (64, 32, 16, 8)
PLANES = (8, 4, 2, 1)
TRANSPOSED = (((1,), (1,)), ((), ()))
NATURAL = (((1,), (0,)), ((), ()))


def split_rows(value):
    high = value.astype(BF16).astype(F32)
    return jnp.concatenate([high, value - high], axis=0).astype(BF16)


def fold_rows(value):
    return value[:8] + value[8:]


def fold_all(value):
    rows = fold_rows(value)
    return rows[:, :128] + rows[:, 128:]


def doubled(value):
    halves = split_rows(value)
    return jnp.concatenate([halves, halves], axis=1)


def matmul(left, right, dims):
    return lax.dot_general(left, right, dims, preferred_element_type=F32)


class Stage:
    def __init__(self):
        self.count = 0

    def take(self):
        self.count += 1
        return self.count - 1


STAGE_COUNT = 48

SCRATCH = dict(
    v0=((128, 8192), F32), v1=((128, 4096), F32), v2=((128, 2048), F32), v3=((128, 1024), F32),
    vp=((3, 1024, 128), F32),
    c0=((64, 256, 128), BF16), c1=((32, 256, 128), BF16), c2=((16, 256, 128), BF16), c3=((8, 256, 128), BF16),
    pc=((3, 1024, 256), BF16),
    rb0=((8, 8, 8, 128), F32), rb1=((4, 8, 8, 128), F32), rb2=((2, 8, 8, 128), F32), rb3=((1, 8, 8, 128), F32),
    tgv=((8, 8, 128), I32),
    up3=((4, 2, 8, 128), F32), up2=((4, 2, 8, 128), F32), up1=((4, 2, 8, 128), F32),
    ur3=((8, 2, 8, 128), F32), ur2=((8, 2, 8, 128), F32), ur1=((8, 2, 8, 128), F32),
    us3=((2, 8, 128), F32), us2=((2, 8, 128), F32), us1=((2, 8, 128), F32),
    uz3=((8, 2, 8, 128), F32), uz2=((8, 2, 8, 128), F32), uz2b=((4, 2, 8, 128), F32), uz1=((8, 2, 8, 128), F32),
    s3p=((2, 8, 8, 128), F32), s3q=((6, 8, 8, 128), F32),
    s2p=((2, 8, 8, 128), F32), s2q=((2, 8, 8, 128), F32), s1p=((2, 8, 8, 128), F32),
    st2=((2, 2, 8, 128), F32), st2b=((2, 2, 8, 128), F32), st1=((2, 2, 8, 128), F32),
    a1=((4, 2, 2, 8, 128), F32), a2=((4, 2, 2, 8, 128), F32), a3=((4, 2, 2, 8, 128), F32),
    ar1=((8, 2, 2, 8, 128), F32), ar2=((8, 2, 2, 8, 128), F32), ar3=((8, 2, 2, 8, 128), F32),
    as1=((2, 2, 8, 128), F32), as2=((2, 2, 8, 128), F32), as3=((2, 2, 8, 128), F32),
    az1=((8, 2, 8, 128), F32), az2=((4, 2, 8, 128), F32), az3=((2, 2, 8, 128), F32),
    pt1=((2, 8, 128), F32), pt2=((2, 8, 128), F32), pt3=((2, 8, 128), F32),
    pk1=((8, 8, 128), F32), pk2=((8, 8, 128), F32), pk3=((8, 8, 128), F32),
    n0=((4, 12, 2, 8, 128), F32), nr0=((8, 12, 2, 8, 128), F32), ns0=((8, 2, 2, 8, 128), F32), nz0=((8, 2, 2, 8, 128), F32),
    n1=((4, 4, 2, 8, 128), F32), nr1=((8, 4, 2, 8, 128), F32), ns1=((4, 2, 8, 128), F32), nz1=((4, 2, 8, 128), F32),
    t0p=((2, 2, 8, 128), F32), t1p=((2, 8, 128), F32),
    sd0=((8, 8, 8, 128), F32), sd1=((8, 4, 8, 128), F32), sd2=((8, 2, 8, 128), F32), sd3=((8, 1, 8, 128), F32),
    dr0=((8, 8, 8, 128), F32), dr1=((8, 4, 8, 128), F32), dr2=((8, 2, 8, 128), F32), dr3=((8, 1, 8, 128), F32),
    ds0=((8, 8, 128), F32), ds1=((4, 8, 128), F32), ds2=((2, 8, 128), F32),
    dz0=((8, 8, 128), F32), dz1=((4, 8, 128), F32), dz2=((2, 8, 128), F32),
    fk=((4, 8, 128), F32),
    dummy=((168, 8, 128), F32),
)


def kernel(rs_ref, i0_ref, i1_ref, i2_ref, i3_ref, pn_ref, tg_ref, fo_ref, so_ref, *scratch):
    names = list(SCRATCH)
    ref = dict(zip(names, scratch[: len(names)]))
    tgs, send_sem, recv_sem, load_sem = scratch[len(names) :]
    front = lax.axis_index("front")
    core = front % 2
    chip_y = (front // 2) % 4
    d = front % 8
    z = front // 8
    is_one = core == 1
    stage = Stage()
    drains = []

    def put(src, dst, st, to):
        pltpu.make_async_remote_copy(
            src_ref=src, dst_ref=dst, send_sem=send_sem.at[st], recv_sem=recv_sem.at[st],
            device_id={"front": to}, device_id_type=MESH,
        ).start()

    def drain(sem, blocks):
        piece = ref["dummy"].at[pl.ds(0, blocks)]
        pltpu.make_async_copy(piece, piece, sem).wait()

    def arrived(st, blocks):
        drain(recv_sem.at[st], blocks)

    def arrived_by_core(st, blocks_zero, blocks_one):
        @pl.when(is_one)
        def _():
            arrived(st, blocks_one)

        @pl.when(jnp.logical_not(is_one))
        def _():
            arrived(st, blocks_zero)

    loads = {}
    for number, (name, src) in enumerate(
        (("v3", i3_ref), ("p3", pn_ref.at[2]), ("v2", i2_ref), ("p2", pn_ref.at[1]),
         ("v1", i1_ref), ("p1", pn_ref.at[0]), ("v0", i0_ref))
    ):
        dst = ref["vp"].at[int(name[1]) - 1] if name[0] == "p" else ref[name]
        loads[name] = pltpu.make_async_copy(src, dst, load_sem.at[number])
        loads[name].start()

    barrier = pltpu.get_barrier_semaphore()
    masks = list(range(1, 16)) + [8 * m for m in range(2, 8)]
    for mask in masks:
        pl.semaphore_signal(barrier, inc=1, device_id={"front": front ^ mask}, device_id_type=MESH)

    rb = [ref["rb0"], ref["rb1"], ref["rb2"], ref["rb3"]]
    zz = [z, z % 4, z % 2, 0]
    for t in range(TIERS):
        rb[t][zz[t], d] = rs_ref[:, t, :]
    lanes = lax.broadcasted_iota(I32, (8, 128), 1)
    own_targets = jnp.full((8, 128), -1, I32)
    for k in range(3):
        for u in range(SLOTS):
            own_targets = jnp.where(lanes == k * 8 + u, tg_ref[k, 0, u], own_targets)
    ref["tgv"][z] = own_targets

    pl.semaphore_wait(barrier, len(masks))

    st_r3 = stage.take()
    for mask in (4, 5, 2, 3, 6, 7, 1):
        put(rb[3].at[0, d], rb[3].at[0, d], st_r3, front ^ mask)
    drains.append((st_r3, 7, 7))
    st_tg = stage.take()
    st_rz = [stage.take() for t in range(3)]
    put(rb[2].at[z % 2, d], rb[2].at[z % 2, d], st_rz[2], front ^ 8)
    drains.append((st_rz[2], 1, 1))
    for m in range(1, 8):
        put(ref["tgv"].at[z], ref["tgv"].at[z], st_tg, front ^ (8 * m))
    drains.append((st_tg, 7, 7))
    for t, count in ((1, 4), (0, 8)):
        for m in range(1, count):
            put(rb[t].at[zz[t], d], rb[t].at[zz[t], d], st_rz[t], front ^ (8 * m))
        drains.append((st_rz[t], count - 1, count - 1))

    cc = [ref["c0"], ref["c1"], ref["c2"], ref["c3"]]
    vv = [ref["v0"], ref["v1"], ref["v2"], ref["v3"]]

    def prepare_inverse(t):
        loads["v" + str(t)].wait()

        def body(e, carry):
            block = vv[t][:, pl.ds(pl.multiple_of(e * 128, 128), 128)]
            high = block.astype(BF16)
            cc[t][e, 0:128, :] = high
            cc[t][e, 128:256, :] = (block - high.astype(F32)).astype(BF16)
            return carry

        lax.fori_loop(0, BLOCKS[t], body, 0)

    def prepare_panel(t):
        loads["p" + str(t)].wait()

        def body(u, carry):
            rows = pl.ds(pl.multiple_of(u * 128, 128), 128)
            block = ref["vp"][t - 1, rows, :]
            high = block.astype(BF16)
            ref["pc"][t - 1, rows, 0:128] = high
            ref["pc"][t - 1, rows, 128:256] = (block - high.astype(F32)).astype(BF16)
            return carry

        lax.fori_loop(0, SLOTS, body, 0)

    def target(m, k, u):
        return tgs[z ^ m, 0, k * 8 + u]

    def dense_forward(t):
        def chunk(index):
            x = jnp.concatenate([rb[t][index, j] for j in range(8)], axis=1)
            w = jnp.concatenate([cc[t][index * 8 + j] for j in range(8)], axis=1)
            return fold_all(matmul(split_rows(x), w, TRANSPOSED))

        if PLANES[t] == 1:
            return chunk(0)
        return lax.fori_loop(0, PLANES[t], lambda i, total: total + chunk(i), jnp.zeros((8, 128), F32))

    def slots_forward(t, k, m, block_of):
        parts, weights = [], []
        for u in range(SLOTS):
            tag = target(m, k, u)
            live = jnp.where((tag >> 6) == t, 1.0, 0.0).astype(F32)
            parts.append(block_of(u) * live)
            weights.append(cc[t][tag & (BLOCKS[t] - 1)])
        x = jnp.concatenate(parts, axis=1)
        w = jnp.concatenate(weights, axis=1)
        return fold_all(matmul(split_rows(x), w, TRANSPOSED))

    def panel_forward(t, value, out):
        terms = fold_rows(matmul(doubled(value), ref["pc"][t - 1], TRANSPOSED))
        for u in range(SLOTS):
            out[u // 2, u % 2] = terms[:, u * 128 : (u + 1) * 128]

    def panel_backward(t, picked):
        x = jnp.concatenate([picked[u] for u in range(SLOTS)], axis=1)
        return fold_all(matmul(split_rows(x), ref["pc"][t - 1], NATURAL))

    def dense_backward(t, value2, out):
        def chunk(index, carry):
            w = jnp.concatenate([cc[t][index * 8 + j] for j in range(8)], axis=1)
            terms = fold_rows(matmul(value2, w, NATURAL))
            for j in range(8):
                out[j, index] = terms[:, j * 128 : (j + 1) * 128]
            return carry

        if PLANES[t] == 1:
            chunk(0, 0)
        else:
            lax.fori_loop(0, PLANES[t], chunk, 0)

    def slots_backward(t, k, m, value2, out, place):
        weights, lives = [], []
        for u in range(SLOTS):
            tag = target(m, k, u)
            lives.append(jnp.where((tag >> 6) == t, 1.0, 0.0).astype(F32))
            weights.append(cc[t][tag & (BLOCKS[t] - 1)])
        w = jnp.concatenate(weights, axis=1)
        terms = fold_rows(matmul(value2, w, NATURAL))
        for u in range(SLOTS):
            out[u // 2, place, u % 2] = terms[:, u * 128 : (u + 1) * 128] * lives[u]

    def reduce_send(out, into, blocks):
        st = stage.take()
        for k in (2, 1, 3):
            put(out.at[chip_y ^ k], into.at[d], st, (front ^ (2 * k)) | 1)

        @pl.when(jnp.logical_not(is_one))
        def _():
            put(out.at[chip_y], into.at[d], st, front ^ 1)

        drains.append((st, 4 * blocks, 3 * blocks))
        return st

    def reduced(st, out, into, blocks, index):
        total = out[(chip_y,) + index]
        for k in range(1, 8):
            total = total + into[(d ^ k,) + index]
        return total

    def spread(src, dst, blocks):
        st = stage.take()
        for mask in (4, 5, 2, 3, 6, 7, 1):
            put(src, dst, st, front ^ mask)
        drains.append((st, 0, 7 * blocks))
        return st

    def on_one(body):
        pl.when(is_one)(body)

    pair = pl.ds(2 * chip_y, 2)

    prepare_inverse(3)
    prepare_panel(3)
    arrived(st_r3, 7)
    forward3 = dense_forward(3)
    panel_forward(3, forward3, ref["up3"])
    st = reduce_send(ref["up3"], ref["ur3"], 2)
    fo_ref[:, 3, :] = forward3
    ref["fk"][3] = forward3
    arrived(st_tg, 7)
    targets_copy = pltpu.make_async_copy(ref["tgv"], tgs, load_sem.at[7])
    targets_copy.start()
    arrived(st_rz[2], 1)
    st_rp = [None] * 3

    def plane_gather(t):
        st_rp[t] = stage.take()
        for mask in (4, 5, 2, 3, 6, 7, 1):
            put(rb[t].at[:, d], rb[t].at[:, d], st_rp[t], front ^ mask)
        drains.append((st_rp[t], 7 * PLANES[t], 7 * PLANES[t]))

    plane_gather(2)
    prepare_inverse(2)
    targets_copy.wait()
    st_s3 = stage.take()
    st_z3 = stage.take()

    @on_one
    def _():
        arrived(st, 14)
        for i in range(2):
            total = reduced(st, ref["up3"], ref["ur3"], 2, (i,))
            ref["us3"][i] = total
            ref["s3p"][0, 2 * chip_y + i] = total
        for mask in (12, 13, 10, 11, 14, 15, 8, 9):
            put(ref["us3"], ref["s3p"].at[1, pair], st_s3, front ^ mask)
        for mask in (4, 5, 2, 3, 6, 7, 1):
            put(ref["us3"], ref["s3p"].at[0, pair], st_s3, front ^ mask)
        for m in range(2, 8):
            put(ref["us3"], ref["uz3"].at[m], st_z3, front ^ (8 * m))

    drains.append((st_s3, 0, 30))
    drains.append((st_z3, 0, 12))
    prepare_panel(2)
    arrived(st_rp[2], 14)
    base2 = dense_forward(2)
    arrived_by_core(st_s3, 16, 14)

    forward2 = base2
    for m in range(2):
        forward2 = forward2 - slots_forward(2, 2, m, lambda u, m=m: ref["s3p"][m, u])
    panel_forward(2, forward2, ref["up2"])
    st = reduce_send(ref["up2"], ref["ur2"], 2)
    fo_ref[:, 2, :] = forward2
    ref["fk"][2] = forward2
    arrived(st_rz[1], 3)
    plane_gather(1)
    prepare_inverse(1)
    st_q3 = stage.take()

    @on_one
    def _():
        arrived(st_z3, 12)
        for m in range(2, 8):
            for i in range(2):
                ref["s3q"][m - 2, 2 * chip_y + i] = ref["uz3"][m, i]
        for mask in (4, 5, 2, 3, 6, 7, 1):
            put(ref["uz3"].at[pl.ds(2, 6)], ref["s3q"].at[:, pair], st_q3, front ^ mask)

    drains.append((st_q3, 0, 84))
    st_z2 = stage.take()
    st_z2b = stage.take()

    @on_one
    def _():
        arrived(st, 14)
        for i in range(2):
            ref["us2"][i] = reduced(st, ref["up2"], ref["ur2"], 2, (i,))
        for m in (2, 3, 1):
            put(ref["us2"], ref["uz2"].at[m], st_z2, front ^ (8 * m))
        for m in range(4, 8):
            put(ref["us2"], ref["uz2b"].at[m - 4], st_z2b, front ^ (8 * m))

    drains.append((st_z2, 0, 6))
    drains.append((st_z2b, 0, 8))
    prepare_panel(1)
    arrived(st_rp[1], 28)
    base1 = dense_forward(1)
    arrived(st_rz[0], 7)
    plane_gather(0)
    st_s2 = stage.take()

    @on_one
    def _():
        arrived(st_z2, 6)
        for i in range(2):
            own = ref["us2"][i] + ref["uz2"][1, i]
            other = ref["uz2"][2, i] + ref["uz2"][3, i]
            for h, total in ((0, own), (1, other)):
                ref["st2"][h, i] = total
                ref["s2p"][h, 2 * chip_y + i] = total
        for mask in (4, 5, 2, 3, 6, 7, 1):
            put(ref["st2"], ref["s2p"].at[:, pair], st_s2, front ^ mask)

    drains.append((st_s2, 0, 28))
    arrived_by_core(st_q3, 48, 36)
    for m in range(4):
        src = ref["s3p"].at[m] if m < 2 else ref["s3q"].at[m - 2]
        base1 = base1 - slots_forward(1, 2, m, lambda u, src=src: src[u])
    arrived_by_core(st_s2, 16, 12)

    forward1 = base1
    for h in range(2):
        forward1 = forward1 - slots_forward(1, 1, 2 * h, lambda u, h=h: ref["s2p"][h, u])
    panel_forward(1, forward1, ref["up1"])
    st = reduce_send(ref["up1"], ref["ur1"], 2)
    fo_ref[:, 1, :] = forward1
    ref["fk"][1] = forward1
    prepare_inverse(0)
    st_z1 = stage.take()

    @on_one
    def _():
        arrived(st, 14)
        for i in range(2):
            ref["us1"][i] = reduced(st, ref["up1"], ref["ur1"], 2, (i,))
        for m in (4, 5, 3, 6, 2, 7, 1):
            put(ref["us1"], ref["uz1"].at[m], st_z1, front ^ (8 * m))

    drains.append((st_z1, 0, 14))
    st_q2 = stage.take()

    @on_one
    def _():
        arrived(st_z2b, 8)
        for i in range(2):
            for h in range(2):
                total = ref["uz2b"][2 * h, i] + ref["uz2b"][2 * h + 1, i]
                ref["st2b"][h, i] = total
                ref["s2q"][h, 2 * chip_y + i] = total
        for mask in (4, 5, 2, 3, 6, 7, 1):
            put(ref["st2b"], ref["s2q"].at[:, pair], st_q2, front ^ mask)

    drains.append((st_q2, 0, 28))
    arrived(st_rp[0], 56)
    base0 = dense_forward(0)
    for h in range(2):
        base0 = base0 - slots_forward(0, 1, 2 * h, lambda u, h=h: ref["s2p"][h, u])
    st_s1 = stage.take()

    @on_one
    def _():
        arrived(st_z1, 14)
        for i in range(2):
            own = ref["us1"][i]
            for m in range(1, 4):
                own = own + ref["uz1"][m, i]
            other = ref["uz1"][4, i]
            for m in range(5, 8):
                other = other + ref["uz1"][m, i]
            for h, total in ((0, own), (1, other)):
                ref["st1"][h, i] = total
                ref["s1p"][h, 2 * chip_y + i] = total
        for mask in (4, 5, 2, 3, 6, 7, 1):
            put(ref["st1"], ref["s1p"].at[:, pair], st_s1, front ^ mask)

    drains.append((st_s1, 0, 28))
    for m in range(2):
        base0 = base0 - slots_forward(0, 2, m, lambda u, m=m: ref["s3p"][m, u])
    base0 = lax.fori_loop(
        0, 6, lambda m, total: total - slots_forward(0, 2, m + 2, lambda u: ref["s3q"][m, u]), base0
    )
    arrived_by_core(st_q2, 16, 12)
    for h in range(2):
        base0 = base0 - slots_forward(0, 1, 4 + 2 * h, lambda u, h=h: ref["s2q"][h, u])
    arrived_by_core(st_s1, 16, 12)

    forward0 = base0
    for h in range(2):
        forward0 = forward0 - slots_forward(0, 0, 4 * h, lambda u, h=h: ref["s1p"][h, u])

    value2 = doubled(forward0)
    for h in range(2):
        slots_backward(0, 0, 4 * h, value2, ref["a1"], h)
    st = reduce_send(ref["a1"], ref["ar1"], 4)
    fo_ref[:, 0, :] = forward0
    dense_backward(0, value2, ref["sd0"])
    for j in range(12):
        k = 1 if j < 4 else 2
        m = 2 * j if j < 4 else j - 4
        for u in range(SLOTS):
            tag = target(m, k, u)
            live = jnp.where((tag >> 6) == 0, 1.0, 0.0).astype(F32)
            ref["n0"][u // 2, j, u % 2] = ref["sd0"][tag & 7, (tag >> 3) & 7] * live
    st_n0 = reduce_send(ref["n0"], ref["nr0"], 24)

    def dense_send(out, into, blocks):
        st_d = stage.take()
        for mask in (4, 5, 2, 3, 6, 7, 1):
            put(out.at[d ^ mask], into.at[mask], st_d, front ^ mask)
        drains.append((st_d, 7 * blocks, 7 * blocks))
        return st_d

    def dense_total(out, into, index):
        total = out[d, index]
        for mask in range(1, 8):
            total = total + into[mask, index]
        return total

    st_d0 = dense_send(ref["sd0"], ref["dr0"], 8)
    st_z = stage.take()

    @on_one
    def _():
        arrived(st, 28)
        for h in range(2):
            for i in range(2):
                ref["as1"][h, i] = reduced(st, ref["a1"], ref["ar1"], 4, (h, i))
        for m in (4, 5, 3, 6, 2, 7, 1):
            put(ref["as1"].at[m >> 2], ref["az1"].at[m], st_z, front ^ (8 * m))

    drains.append((st_z, 0, 14))
    st_p = stage.take()

    @on_one
    def _():
        arrived(st_z, 14)
        for i in range(2):
            total = ref["as1"][0, i]
            for m in range(1, 8):
                total = total + ref["az1"][m, i]
            ref["pt1"][i] = total
            ref["pk1"][2 * chip_y + i] = total
        for mask in (4, 5, 2, 3, 6, 7, 1):
            put(ref["pt1"], ref["pk1"].at[pair], st_p, front ^ mask)

    drains.append((st_p, 0, 14))
    st_nz0 = stage.take()

    @on_one
    def _():
        arrived(st_n0, 168)

        def body(m, carry):
            for i in range(2):
                ref["ns0"][m, 0, i] = reduced(st_n0, ref["n0"], ref["nr0"], 24, (m // 2, i))
                ref["ns0"][m, 1, i] = reduced(st_n0, ref["n0"], ref["nr0"], 24, (4 + m, i))
            return carry

        lax.fori_loop(0, 8, body, 0)
        for m in range(1, 8):
            put(ref["ns0"].at[m], ref["nz0"].at[m], st_nz0, front ^ (8 * m))

    drains.append((st_nz0, 0, 28))
    arrived_by_core(st_p, 8, 6)

    value2 = doubled(ref["fk"][1] - panel_backward(1, ref["pk1"]))
    for h in range(2):
        slots_backward(1, 1, 2 * h, value2, ref["a2"], h)
    st = reduce_send(ref["a2"], ref["ar2"], 4)
    dense_backward(1, value2, ref["sd1"])
    for m in range(4):
        for u in range(SLOTS):
            tag = target(m, 2, u)
            live = jnp.where((tag >> 6) == 1, 1.0, 0.0).astype(F32)
            ref["n1"][u // 2, m, u % 2] = ref["sd1"][tag & 7, (tag >> 3) & 3] * live
    st_n1 = reduce_send(ref["n1"], ref["nr1"], 8)
    st_d1 = dense_send(ref["sd1"], ref["dr1"], 4)

    st_z = stage.take()

    @on_one
    def _():
        arrived(st, 28)
        for h in range(2):
            for i in range(2):
                ref["as2"][h, i] = reduced(st, ref["a2"], ref["ar2"], 4, (h, i))
        for m in (2, 3, 1):
            put(ref["as2"].at[m >> 1], ref["az2"].at[m], st_z, front ^ (8 * m))

    drains.append((st_z, 0, 6))

    @on_one
    def _():
        arrived(st_nz0, 28)
        for q in range(2):
            for i in range(2):
                total = ref["ns0"][0, q, i]
                for m in range(1, 8):
                    total = total + ref["nz0"][m, q, i]
                ref["t0p"][q, i] = total

    st_p = stage.take()

    @on_one
    def _():
        arrived(st_z, 6)
        for i in range(2):
            total = ref["as2"][0, i] + ref["t0p"][0, i]
            for m in range(1, 4):
                total = total + ref["az2"][m, i]
            ref["pt2"][i] = total
            ref["pk2"][2 * chip_y + i] = total
        for mask in (4, 5, 2, 3, 6, 7, 1):
            put(ref["pt2"], ref["pk2"].at[pair], st_p, front ^ mask)

    drains.append((st_p, 0, 14))
    st_nz1 = stage.take()

    @on_one
    def _():
        arrived(st_n1, 56)
        for m in range(4):
            for i in range(2):
                ref["ns1"][m, i] = reduced(st_n1, ref["n1"], ref["nr1"], 8, (m, i))
        for m in range(1, 4):
            put(ref["ns1"].at[m], ref["nz1"].at[m], st_nz1, front ^ (8 * m))

    drains.append((st_nz1, 0, 6))

    st_dz0 = stage.take()
    arrived(st_d0, 56)
    for w in range(8):
        ref["ds0"][w] = dense_total(ref["sd0"], ref["dr0"], w)
    for m in range(1, 8):
        put(ref["ds0"].at[z ^ m], ref["dz0"].at[m], st_dz0, front ^ (8 * m))
    drains.append((st_dz0, 7, 7))
    arrived_by_core(st_p, 8, 6)

    value2 = doubled(ref["fk"][2] - panel_backward(2, ref["pk2"]))
    for h in range(2):
        slots_backward(2, 2, h, value2, ref["a3"], h)
    st = reduce_send(ref["a3"], ref["ar3"], 4)
    dense_backward(2, value2, ref["sd2"])
    st_d2 = dense_send(ref["sd2"], ref["dr2"], 2)

    st_z = stage.take()

    @on_one
    def _():
        arrived(st, 28)
        for h in range(2):
            for i in range(2):
                ref["as3"][h, i] = reduced(st, ref["a3"], ref["ar3"], 4, (h, i))
        put(ref["as3"].at[1], ref["az3"].at[1], st_z, front ^ 8)

    drains.append((st_z, 0, 2))

    @on_one
    def _():
        arrived(st_nz1, 6)
        for i in range(2):
            total = ref["ns1"][0, i] + ref["t0p"][1, i]
            for m in range(1, 4):
                total = total + ref["nz1"][m, i]
            ref["t1p"][i] = total

    st_p = stage.take()

    @on_one
    def _():
        arrived(st_z, 2)
        for i in range(2):
            total = ref["as3"][0, i] + ref["t1p"][i] + ref["az3"][1, i]
            ref["pt3"][i] = total
            ref["pk3"][2 * chip_y + i] = total
        for mask in (4, 5, 2, 3, 6, 7, 1):
            put(ref["pt3"], ref["pk3"].at[pair], st_p, front ^ mask)

    drains.append((st_p, 0, 14))
    st_dz1 = stage.take()
    arrived(st_d1, 28)
    for w in range(4):
        ref["ds1"][w] = dense_total(ref["sd1"], ref["dr1"], w)
    for m in range(1, 4):
        put(ref["ds1"].at[(z ^ m) % 4], ref["dz1"].at[m], st_dz1, front ^ (8 * m))
    drains.append((st_dz1, 3, 3))
    st_dz2 = stage.take()
    arrived(st_d2, 14)
    for w in range(2):
        ref["ds2"][w] = dense_total(ref["sd2"], ref["dr2"], w)
    put(ref["ds2"].at[(z ^ 1) % 2], ref["dz2"].at[1], st_dz2, front ^ 8)
    drains.append((st_dz2, 1, 1))
    arrived(st_dz0, 7)
    total = ref["ds0"][z]
    for m in range(1, 8):
        total = total + ref["dz0"][m]
    so_ref[:, 0, :] = total
    arrived_by_core(st_p, 8, 6)

    value2 = doubled(ref["fk"][3] - panel_backward(3, ref["pk3"]))
    dense_backward(3, value2, ref["sd3"])
    st_d3 = dense_send(ref["sd3"], ref["dr3"], 1)
    arrived(st_dz1, 3)
    total = ref["ds1"][z % 4]
    for m in range(1, 4):
        total = total + ref["dz1"][m]
    so_ref[:, 1, :] = total
    arrived(st_dz2, 1)
    so_ref[:, 2, :] = ref["ds2"][z % 2] + ref["dz2"][1]

    @on_one
    def _():
        for st_x, _zero, one in drains:
            left = one
            while left:
                drain(send_sem.at[st_x], min(left, 168))
                left -= min(left, 168)

    @pl.when(jnp.logical_not(is_one))
    def _():
        for st_x, zero, _one in drains:
            left = zero
            while left:
                drain(send_sem.at[st_x], min(left, 168))
                left -= min(left, 168)

    arrived(st_d3, 7)
    so_ref[:, 3, :] = dense_total(ref["sd3"], ref["dr3"], 0)
    assert stage.count <= STAGE_COUNT


def shards(right_side, inverse_top, inverse_second, inverse_third, inverse_fourth, panels, targets):
    vmem = pl.BlockSpec(memory_space=pltpu.VMEM)
    anywhere = pl.BlockSpec(memory_space=pl.ANY)
    smem = pl.BlockSpec(memory_space=pltpu.SMEM)
    out = jax.ShapeDtypeStruct(right_side.shape, F32)
    return pl.pallas_call(
        kernel,
        out_shape=(out, out),
        in_specs=[vmem, anywhere, anywhere, anywhere, anywhere, anywhere, smem],
        out_specs=(vmem, vmem),
        scratch_shapes=[pltpu.VMEM(shape, dtype) for shape, dtype in SCRATCH.values()]
        + [
            pltpu.SMEM((8, 8, 128), I32),
            pltpu.SemaphoreType.DMA((STAGE_COUNT,)),
            pltpu.SemaphoreType.DMA((STAGE_COUNT,)),
            pltpu.SemaphoreType.DMA((8,)),
        ],
        compiler_params=pltpu.CompilerParams(
            collective_id=0, has_side_effects=True, vmem_limit_bytes=56 * 2**20
        ),
        name="tiers",
    )(right_side, inverse_top, inverse_second, inverse_third, inverse_fourth, panels, targets)


def solution(mesh):
    placed = (
        P("rhs", None, "front"),
        P("front", None),
        P("front", None),
        P("front", None),
        P("front", None),
        P(None, None, "front"),
        P(None, "front", None),
    )
    return jax.shard_map(
        shards,
        mesh=mesh,
        in_specs=placed,
        out_specs=(P("rhs", None, "front"), P("rhs", None, "front")),
        check_vma=False,
    )
```

profile of v0, /device:TPU:1, one launch (start us, length us, event | category | flops | bytes accessed | tf_op | source)
XLA Modules:
  0.0 82.9 jit_solution(16309623785876853933)
XLA Ops:
  0.6 79.6 %tiers.1 = (f32[8,4,128]{2,1,0:T(4,128)}, f32[8,4,128]{2,1,0:T(4,128)}) custom-call(f32[8,4,128]{2,1,0:T(4,128)} %rs_ref.1, f32[128,8192]{1,0:T(8,128)} %i0_ref.1, f32[128,4096]{1,0:T(8,128)} %i1_ref.1, f32[128,2048]{1,0:T(8,128)} %i2_ref.1, f32[128,1024]{1,0:T(8,128)} %i3_ref.1, f32[3,1024,128]{2,1,0:T(8,128)} %pn_ref.1, s32[3,1,8]{2,1,0:T(1,128)} %tg_ref.1), custom_call_target="tpu_custom_call" | custom-call | tf_op jit(solution)/shard_map/tiers/pallas_call | solution.py:707
  80.3 1.3 %copy.11 = f32[8,4,128]{2,1,0:T(4,128)} copy(f32[8,4,128]{2,1,0:T(4,128)} %get-tuple-element.4) | data formatting | bytes 32768
  81.6 1.3 %copy.12 = f32[8,4,128]{2,1,0:T(4,128)} copy(f32[8,4,128]{2,1,0:T(4,128)} %get-tuple-element.5) | data formatting | bytes 32768
where the time goes:
time: 83.3 us; the launch traced here: 82.9 us
  Pallas kernels  79.6 us (96%)
  local copies, waits for them, and re-layouts  2.65 us (3%)
    pallas_call x1, Pallas kernels, shards(): pl.pallas_call(kernel, out_shape=(out, out), in_specs=[vmem, anywhere, an...  79.6 us
    unnamed x2, local copies, waits for them, and re-layouts  2.65 us

commit v1 on v0

--- a/solution.py
+++ b/solution.py
@@ -58,37 +58,40 @@
     vp=((3, 1024, 128), F32),
     c0=((64, 256, 128), BF16), c1=((32, 256, 128), BF16), c2=((16, 256, 128), BF16), c3=((8, 256, 128), BF16),
     pc=((3, 1024, 256), BF16),
-    rb0=((8, 8, 8, 128), F32), rb1=((4, 8, 8, 128), F32), rb2=((2, 8, 8, 128), F32), rb3=((1, 8, 8, 128), F32),
+    rb0=((8, 2, 4, 8, 128), F32), rb1=((4, 2, 4, 8, 128), F32), rb2=((2, 2, 4, 8, 128), F32), rb3=((1, 2, 4, 8, 128), F32),
     tgv=((8, 8, 128), I32),
     up3=((4, 2, 8, 128), F32), up2=((4, 2, 8, 128), F32), up1=((4, 2, 8, 128), F32),
     ur3=((8, 2, 8, 128), F32), ur2=((8, 2, 8, 128), F32), ur1=((8, 2, 8, 128), F32),
     us3=((2, 8, 128), F32), us2=((2, 8, 128), F32), us1=((2, 8, 128), F32),
     uz3=((8, 2, 8, 128), F32), uz2=((8, 2, 8, 128), F32), uz2b=((4, 2, 8, 128), F32), uz1=((8, 2, 8, 128), F32),
-    s3p=((2, 8, 8, 128), F32), s3q=((6, 8, 8, 128), F32),
+    s3p=((2, 8, 8, 128), F32), s3q=((2, 8, 8, 128), F32), s3r=((4, 8, 8, 128), F32),
     s2p=((2, 8, 8, 128), F32), s2q=((2, 8, 8, 128), F32), s1p=((2, 8, 8, 128), F32),
     st2=((2, 2, 8, 128), F32), st2b=((2, 2, 8, 128), F32), st1=((2, 2, 8, 128), F32),
     a1=((4, 2, 2, 8, 128), F32), a2=((4, 2, 2, 8, 128), F32), a3=((4, 2, 2, 8, 128), F32),
     ar1=((8, 2, 2, 8, 128), F32), ar2=((8, 2, 2, 8, 128), F32), ar3=((8, 2, 2, 8, 128), F32),
     as1=((2, 2, 8, 128), F32), as2=((2, 2, 8, 128), F32), as3=((2, 2, 8, 128), F32),
-    az1=((8, 2, 8, 128), F32), az2=((4, 2, 8, 128), F32), az3=((2, 2, 8, 128), F32),
+    az1=((8, 2, 8, 128), F32), az2=((4, 2, 8, 128), F32),
     pt1=((2, 8, 128), F32), pt2=((2, 8, 128), F32), pt3=((2, 8, 128), F32),
-    pk1=((8, 8, 128), F32), pk2=((8, 8, 128), F32), pk3=((8, 8, 128), F32),
-    n0=((4, 12, 2, 8, 128), F32), nr0=((8, 12, 2, 8, 128), F32), ns0=((8, 2, 2, 8, 128), F32), nz0=((8, 2, 2, 8, 128), F32),
+    pk1=((8, 8, 128), F32), pk2=((8, 8, 128), F32), pk3=((2, 8, 8, 128), F32),
+    n0=((4, 12, 2, 8, 128), F32), nx0=((4, 12, 2, 8, 128), F32), ne0=((4, 12, 2, 8, 128), F32), nr0=((4, 12, 2, 8, 128), F32), ns0=((8, 2, 2, 8, 128), F32), nz0=((8, 2, 2, 8, 128), F32),
     n1=((4, 4, 2, 8, 128), F32), nr1=((8, 4, 2, 8, 128), F32), ns1=((4, 2, 8, 128), F32), nz1=((4, 2, 8, 128), F32),
     t0p=((2, 2, 8, 128), F32), t1p=((2, 8, 128), F32),
-    sd0=((8, 8, 8, 128), F32), sd1=((8, 4, 8, 128), F32), sd2=((8, 2, 8, 128), F32), sd3=((8, 1, 8, 128), F32),
-    dr0=((8, 8, 8, 128), F32), dr1=((8, 4, 8, 128), F32), dr2=((8, 2, 8, 128), F32), dr3=((8, 1, 8, 128), F32),
+    sd0=((2, 4, 8, 8, 128), F32), sd1=((2, 4, 4, 8, 128), F32), sd2=((2, 4, 2, 8, 128), F32), sd3=((2, 4, 1, 8, 128), F32),
+    dx0=((4, 8, 8, 128), F32), dx1=((4, 4, 8, 128), F32), de0=((4, 8, 8, 128), F32), de1=((4, 4, 8, 128), F32),
+    dr0=((4, 8, 8, 128), F32), dr1=((4, 4, 8, 128), F32), dr2=((8, 2, 8, 128), F32), dr3=((8, 1, 8, 128), F32),
     ds0=((8, 8, 128), F32), ds1=((4, 8, 128), F32), ds2=((2, 8, 128), F32),
     dz0=((8, 8, 128), F32), dz1=((4, 8, 128), F32), dz2=((2, 8, 128), F32),
     fk=((4, 8, 128), F32),
+    rs=((8, 4, 128), F32),
     dummy=((168, 8, 128), F32),
 )
 
 
-def kernel(rs_ref, i0_ref, i1_ref, i2_ref, i3_ref, pn_ref, tg_ref, fo_ref, so_ref, *scratch):
+def kernel(rs_hbm, i0_ref, i1_ref, i2_ref, i3_ref, pn_ref, tg_hbm, out_ref, *scratch):
     names = list(SCRATCH)
     ref = dict(zip(names, scratch[: len(names)]))
-    tgs, send_sem, recv_sem, load_sem = scratch[len(names) :]
+    tgs, tg_ref, send_sem, recv_sem, load_sem = scratch[len(names) :]
+    rs_ref, fo_ref, so_ref = ref["rs"], out_ref.at[0], out_ref.at[1]
     front = lax.axis_index("front")
     core = front % 2
     chip_y = (front // 2) % 4
@@ -120,7 +123,16 @@
         def _():
             arrived(st, blocks_zero)
 
+    barrier = pltpu.get_barrier_semaphore()
+    masks = list(range(1, 16)) + [8 * m for m in range(2, 8)]
+    for mask in masks:
+        pl.semaphore_signal(barrier, inc=1, device_id={"front": front ^ mask}, device_id_type=MESH)
+
     loads = {}
+    rs_copy = pltpu.make_async_copy(rs_hbm, rs_ref, load_sem.at[8])
+    rs_copy.start()
+    tg_copy = pltpu.make_async_copy(tg_hbm, tg_ref, load_sem.at[9])
+    tg_copy.start()
     for number, (name, src) in enumerate(
         (("v3", i3_ref), ("p3", pn_ref.at[2]), ("v2", i2_ref), ("p2", pn_ref.at[1]),
          ("v1", i1_ref), ("p1", pn_ref.at[0]), ("v0", i0_ref))
@@ -129,15 +141,12 @@
         loads[name] = pltpu.make_async_copy(src, dst, load_sem.at[number])
         loads[name].start()
 
-    barrier = pltpu.get_barrier_semaphore()
-    masks = list(range(1, 16)) + [8 * m for m in range(2, 8)]
-    for mask in masks:
-        pl.semaphore_signal(barrier, inc=1, device_id={"front": front ^ mask}, device_id_type=MESH)
-
+    rs_copy.wait()
+    tg_copy.wait()
     rb = [ref["rb0"], ref["rb1"], ref["rb2"], ref["rb3"]]
     zz = [z, z % 4, z % 2, 0]
     for t in range(TIERS):
-        rb[t][zz[t], d] = rs_ref[:, t, :]
+        rb[t][zz[t], core, chip_y] = rs_ref[:, t, :]
     lanes = lax.broadcasted_iota(I32, (8, 128), 1)
     own_targets = jnp.full((8, 128), -1, I32)
     for k in range(3):
@@ -149,18 +158,18 @@
 
     st_r3 = stage.take()
     for mask in (4, 5, 2, 3, 6, 7, 1):
-        put(rb[3].at[0, d], rb[3].at[0, d], st_r3, front ^ mask)
+        put(rb[3].at[0, core, chip_y], rb[3].at[0, core, chip_y], st_r3, front ^ mask)
     drains.append((st_r3, 7, 7))
     st_tg = stage.take()
     st_rz = [stage.take() for t in range(3)]
-    put(rb[2].at[z % 2, d], rb[2].at[z % 2, d], st_rz[2], front ^ 8)
+    put(rb[2].at[z % 2, core, chip_y], rb[2].at[z % 2, core, chip_y], st_rz[2], front ^ 8)
     drains.append((st_rz[2], 1, 1))
     for m in range(1, 8):
         put(ref["tgv"].at[z], ref["tgv"].at[z], st_tg, front ^ (8 * m))
     drains.append((st_tg, 7, 7))
     for t, count in ((1, 4), (0, 8)):
         for m in range(1, count):
-            put(rb[t].at[zz[t], d], rb[t].at[zz[t], d], st_rz[t], front ^ (8 * m))
+            put(rb[t].at[zz[t], core, chip_y], rb[t].at[zz[t], core, chip_y], st_rz[t], front ^ (8 * m))
         drains.append((st_rz[t], count - 1, count - 1))
 
     cc = [ref["c0"], ref["c1"], ref["c2"], ref["c3"]]
@@ -196,7 +205,7 @@
 
     def dense_forward(t):
         def chunk(index):
-            x = jnp.concatenate([rb[t][index, j] for j in range(8)], axis=1)
+            x = jnp.concatenate([rb[t][index, j % 2, j // 2] for j in range(8)], axis=1)
             w = jnp.concatenate([cc[t][index * 8 + j] for j in range(8)], axis=1)
             return fold_all(matmul(split_rows(x), w, TRANSPOSED))
 
@@ -229,7 +238,7 @@
             w = jnp.concatenate([cc[t][index * 8 + j] for j in range(8)], axis=1)
             terms = fold_rows(matmul(value2, w, NATURAL))
             for j in range(8):
-                out[j, index] = terms[:, j * 128 : (j + 1) * 128]
+                out[j % 2, j // 2, index] = terms[:, j * 128 : (j + 1) * 128]
             return carry
 
         if PLANES[t] == 1:
@@ -291,12 +300,19 @@
     targets_copy.start()
     arrived(st_rz[2], 1)
     st_rp = [None] * 3
+    st_rc = [None] * 3
 
     def plane_gather(t):
         st_rp[t] = stage.take()
-        for mask in (4, 5, 2, 3, 6, 7, 1):
-            put(rb[t].at[:, d], rb[t].at[:, d], st_rp[t], front ^ mask)
-        drains.append((st_rp[t], 7 * PLANES[t], 7 * PLANES[t]))
+        for mask in (4, 2, 6):
+            put(rb[t].at[:, core, chip_y], rb[t].at[:, core, chip_y], st_rp[t], front ^ mask)
+        drains.append((st_rp[t], 3 * PLANES[t], 3 * PLANES[t]))
+
+    def core_gather(t):
+        arrived(st_rp[t], 3 * PLANES[t])
+        st_rc[t] = stage.take()
+        put(rb[t].at[:, core], rb[t].at[:, core], st_rc[t], front ^ 1)
+        drains.append((st_rc[t], 4 * PLANES[t], 4 * PLANES[t]))
 
     plane_gather(2)
     prepare_inverse(2)
@@ -320,8 +336,9 @@
 
     drains.append((st_s3, 0, 30))
     drains.append((st_z3, 0, 12))
+    core_gather(2)
     prepare_panel(2)
-    arrived(st_rp[2], 14)
+    arrived(st_rc[2], 8)
     base2 = dense_forward(2)
     arrived_by_core(st_s3, 16, 14)
 
@@ -341,12 +358,13 @@
     def _():
         arrived(st_z3, 12)
         for m in range(2, 8):
+            into = ref["s3q"] if m < 4 else ref["s3r"]
             for i in range(2):
-                ref["s3q"][m - 2, 2 * chip_y + i] = ref["uz3"][m, i]
-        for mask in (4, 5, 2, 3, 6, 7, 1):
-            put(ref["uz3"].at[pl.ds(2, 6)], ref["s3q"].at[:, pair], st_q3, front ^ mask)
-
-    drains.append((st_q3, 0, 84))
+                into[m % 2 if m < 4 else m - 4, 2 * chip_y + i] = ref["uz3"][m, i]
+        for mask in (4, 2, 6):
+            put(ref["uz3"].at[pl.ds(2, 2)], ref["s3q"].at[:, pair], st_q3, front ^ mask)
+
+    drains.append((st_q3, 0, 12))
     st_z2 = stage.take()
     st_z2b = stage.take()
 
@@ -362,11 +380,18 @@
 
     drains.append((st_z2, 0, 6))
     drains.append((st_z2b, 0, 8))
+    core_gather(1)
+    st_q3c = stage.take()
+
+    @on_one
+    def _():
+        arrived(st_q3, 12)
+        put(ref["s3q"], ref["s3q"], st_q3c, front ^ 1)
+
+    drains.append((st_q3c, 0, 16))
     prepare_panel(1)
-    arrived(st_rp[1], 28)
+    arrived(st_rc[1], 16)
     base1 = dense_forward(1)
-    arrived(st_rz[0], 7)
-    plane_gather(0)
     st_s2 = stage.take()
 
     @on_one
@@ -382,7 +407,11 @@
             put(ref["st2"], ref["s2p"].at[:, pair], st_s2, front ^ mask)
 
     drains.append((st_s2, 0, 28))
-    arrived_by_core(st_q3, 48, 36)
+
+    @pl.when(jnp.logical_not(is_one))
+    def _():
+        arrived(st_q3c, 16)
+
     for m in range(4):
         src = ref["s3p"].at[m] if m < 2 else ref["s3q"].at[m - 2]
         base1 = base1 - slots_forward(1, 2, m, lambda u, src=src: src[u])
@@ -395,19 +424,8 @@
     st = reduce_send(ref["up1"], ref["ur1"], 2)
     fo_ref[:, 1, :] = forward1
     ref["fk"][1] = forward1
-    prepare_inverse(0)
-    st_z1 = stage.take()
-
-    @on_one
-    def _():
-        arrived(st, 14)
-        for i in range(2):
-            ref["us1"][i] = reduced(st, ref["up1"], ref["ur1"], 2, (i,))
-        for m in (4, 5, 3, 6, 2, 7, 1):
-            put(ref["us1"], ref["uz1"].at[m], st_z1, front ^ (8 * m))
-
-    drains.append((st_z1, 0, 14))
     st_q2 = stage.take()
+    st_r3x = stage.take()
 
     @on_one
     def _():
@@ -419,12 +437,42 @@
                 ref["s2q"][h, 2 * chip_y + i] = total
         for mask in (4, 5, 2, 3, 6, 7, 1):
             put(ref["st2b"], ref["s2q"].at[:, pair], st_q2, front ^ mask)
+        for mask in (4, 2, 6):
+            put(ref["uz3"].at[pl.ds(4, 4)], ref["s3r"].at[:, pair], st_r3x, front ^ mask)
 
     drains.append((st_q2, 0, 28))
-    arrived(st_rp[0], 56)
-    base0 = dense_forward(0)
+    drains.append((st_r3x, 0, 24))
+    arrived(st_rz[0], 7)
+    plane_gather(0)
+    prepare_inverse(0)
+    st_z1 = stage.take()
+
+    @on_one
+    def _():
+        arrived(st, 14)
+        for i in range(2):
+            ref["us1"][i] = reduced(st, ref["up1"], ref["ur1"], 2, (i,))
+        for m in (4, 5, 3, 6, 2, 7, 1):
+            put(ref["us1"], ref["uz1"].at[m], st_z1, front ^ (8 * m))
+
+    drains.append((st_z1, 0, 14))
+    core_gather(0)
+    st_r3c = stage.take()
+
+    @on_one
+    def _():
+        arrived(st_r3x, 24)
+        put(ref["s3r"], ref["s3r"], st_r3c, front ^ 1)
+
+    drains.append((st_r3c, 0, 32))
+    base0 = jnp.zeros((8, 128), F32)
     for h in range(2):
         base0 = base0 - slots_forward(0, 1, 2 * h, lambda u, h=h: ref["s2p"][h, u])
+    for m in range(4):
+        src = ref["s3p"].at[m] if m < 2 else ref["s3q"].at[m - 2]
+        base0 = base0 - slots_forward(0, 2, m, lambda u, src=src: src[u])
+    arrived(st_rc[0], 32)
+    base0 = base0 + dense_forward(0)
     st_s1 = stage.take()
 
     @on_one
@@ -444,10 +492,13 @@
             put(ref["st1"], ref["s1p"].at[:, pair], st_s1, front ^ mask)
 
     drains.append((st_s1, 0, 28))
-    for m in range(2):
-        base0 = base0 - slots_forward(0, 2, m, lambda u, m=m: ref["s3p"][m, u])
+
+    @pl.when(jnp.logical_not(is_one))
+    def _():
+        arrived(st_r3c, 32)
+
     base0 = lax.fori_loop(
-        0, 6, lambda m, total: total - slots_forward(0, 2, m + 2, lambda u: ref["s3q"][m, u]), base0
+        0, 4, lambda m, total: total - slots_forward(0, 2, m + 4, lambda u: ref["s3r"][m, u]), base0
     )
     arrived_by_core(st_q2, 16, 12)
     for h in range(2):
@@ -470,23 +521,55 @@
         for u in range(SLOTS):
             tag = target(m, k, u)
             live = jnp.where((tag >> 6) == 0, 1.0, 0.0).astype(F32)
-            ref["n0"][u // 2, j, u % 2] = ref["sd0"][tag & 7, (tag >> 3) & 7] * live
-    st_n0 = reduce_send(ref["n0"], ref["nr0"], 24)
+            ref["n0"][u // 2, j, u % 2] = ref["sd0"][tag & 1, (tag >> 1) & 3, (tag >> 3) & 7] * live
+    st_nx = stage.take()
+
+    @pl.when(jnp.logical_not(is_one))
+    def _():
+        put(ref["n0"], ref["nx0"], st_nx, front ^ 1)
+
+    drains.append((st_nx, 96, 0))
 
     def dense_send(out, into, blocks):
         st_d = stage.take()
         for mask in (4, 5, 2, 3, 6, 7, 1):
-            put(out.at[d ^ mask], into.at[mask], st_d, front ^ mask)
+            put(out.at[core ^ (mask & 1), chip_y ^ (mask >> 1)], into.at[mask], st_d, front ^ mask)
         drains.append((st_d, 7 * blocks, 7 * blocks))
         return st_d
 
     def dense_total(out, into, index):
-        total = out[d, index]
+        total = out[core, chip_y, index]
         for mask in range(1, 8):
             total = total + into[mask, index]
         return total
 
-    st_d0 = dense_send(ref["sd0"], ref["dr0"], 8)
+    def chip_send(out, into, blocks):
+        st_x = stage.take()
+        put(out.at[1 - core], into, st_x, front ^ 1)
+        drains.append((st_x, 4 * blocks, 4 * blocks))
+        return st_x
+
+    def chip_total_send(st_x, out, cross, summed, into, blocks):
+        arrived(st_x, 4 * blocks)
+
+        def body(w, carry):
+            for y in range(4):
+                summed[y, w] = out[core, y, w] + cross[y, w]
+            return carry
+
+        lax.fori_loop(0, blocks, body, 0)
+        st_d = stage.take()
+        for k in (2, 1, 3):
+            put(summed.at[chip_y ^ k], into.at[k], st_d, front ^ (2 * k))
+        drains.append((st_d, 3 * blocks, 3 * blocks))
+        return st_d
+
+    def plane_total(st_d, summed, into, final, blocks):
+        arrived(st_d, 3 * blocks)
+        for w in range(blocks):
+            final[w] = (summed[chip_y, w] + into[1, w]) + (into[2, w] + into[3, w])
+
+    st_dx0 = chip_send(ref["sd0"], ref["dx0"], 8)
     st_z = stage.take()
 
     @on_one
@@ -499,6 +582,24 @@
             put(ref["as1"].at[m >> 2], ref["az1"].at[m], st_z, front ^ (8 * m))
 
     drains.append((st_z, 0, 14))
+    st_n0 = stage.take()
+
+    @on_one
+    def _():
+        arrived(st_nx, 96)
+
+        def body(j, carry):
+            for y in range(4):
+                for i in range(2):
+                    ref["ne0"][y, j, i] = ref["n0"][y, j, i] + ref["nx0"][y, j, i]
+            return carry
+
+        lax.fori_loop(0, 12, body, 0)
+        for k in (2, 1, 3):
+            put(ref["ne0"].at[chip_y ^ k], ref["nr0"].at[k], st_n0, front ^ (2 * k))
+
+    drains.append((st_n0, 0, 72))
+    st_d0 = chip_total_send(st_dx0, ref["sd0"], ref["dx0"], ref["de0"], ref["dr0"], 8)
     st_p = stage.take()
 
     @on_one
@@ -518,12 +619,15 @@
 
     @on_one
     def _():
-        arrived(st_n0, 168)
+        arrived(st_n0, 72)
+
+        def total_of(j, i):
+            return (ref["ne0"][chip_y, j, i] + ref["nr0"][1, j, i]) + (ref["nr0"][2, j, i] + ref["nr0"][3, j, i])
 
         def body(m, carry):
             for i in range(2):
-                ref["ns0"][m, 0, i] = reduced(st_n0, ref["n0"], ref["nr0"], 24, (m // 2, i))
-                ref["ns0"][m, 1, i] = reduced(st_n0, ref["n0"], ref["nr0"], 24, (4 + m, i))
+                ref["ns0"][m, 0, i] = total_of(m // 2, i)
+                ref["ns0"][m, 1, i] = total_of(4 + m, i)
             return carry
 
         lax.fori_loop(0, 8, body, 0)
@@ -531,6 +635,11 @@
             put(ref["ns0"].at[m], ref["nz0"].at[m], st_nz0, front ^ (8 * m))
 
     drains.append((st_nz0, 0, 28))
+    st_dz0 = stage.take()
+    plane_total(st_d0, ref["de0"], ref["dr0"], ref["ds0"], 8)
+    for m in range(1, 8):
+        put(ref["ds0"].at[z ^ m], ref["dz0"].at[m], st_dz0, front ^ (8 * m))
+    drains.append((st_dz0, 7, 7))
     arrived_by_core(st_p, 8, 6)
 
     value2 = doubled(ref["fk"][1] - panel_backward(1, ref["pk1"]))
@@ -542,9 +651,9 @@
         for u in range(SLOTS):
             tag = target(m, 2, u)
             live = jnp.where((tag >> 6) == 1, 1.0, 0.0).astype(F32)
-            ref["n1"][u // 2, m, u % 2] = ref["sd1"][tag & 7, (tag >> 3) & 3] * live
+            ref["n1"][u // 2, m, u % 2] = ref["sd1"][tag & 1, (tag >> 1) & 3, (tag >> 3) & 3] * live
     st_n1 = reduce_send(ref["n1"], ref["nr1"], 8)
-    st_d1 = dense_send(ref["sd1"], ref["dr1"], 4)
+    st_dx1 = chip_send(ref["sd1"], ref["dx1"], 4)
 
     st_z = stage.take()
 
@@ -569,6 +678,7 @@
                     total = total + ref["nz0"][m, q, i]
                 ref["t0p"][q, i] = total
 
+    st_d1 = chip_total_send(st_dx1, ref["sd1"], ref["dx1"], ref["de1"], ref["dr1"], 4)
     st_p = stage.take()
 
     @on_one
@@ -597,13 +707,11 @@
 
     drains.append((st_nz1, 0, 6))
 
-    st_dz0 = stage.take()
-    arrived(st_d0, 56)
-    for w in range(8):
-        ref["ds0"][w] = dense_total(ref["sd0"], ref["dr0"], w)
+    arrived(st_dz0, 7)
+    total = ref["ds0"][z]
     for m in range(1, 8):
-        put(ref["ds0"].at[z ^ m], ref["dz0"].at[m], st_dz0, front ^ (8 * m))
-    drains.append((st_dz0, 7, 7))
+        total = total + ref["dz0"][m]
+    so_ref[:, 0, :] = total
     arrived_by_core(st_p, 8, 6)
 
     value2 = doubled(ref["fk"][2] - panel_backward(2, ref["pk2"]))
@@ -613,17 +721,12 @@
     dense_backward(2, value2, ref["sd2"])
     st_d2 = dense_send(ref["sd2"], ref["dr2"], 2)
 
-    st_z = stage.take()
-
-    @on_one
-    def _():
-        arrived(st, 28)
-        for h in range(2):
-            for i in range(2):
-                ref["as3"][h, i] = reduced(st, ref["a3"], ref["ar3"], 4, (h, i))
-        put(ref["as3"].at[1], ref["az3"].at[1], st_z, front ^ 8)
-
-    drains.append((st_z, 0, 2))
+    st_dz1 = stage.take()
+    plane_total(st_d1, ref["de1"], ref["dr1"], ref["ds1"], 4)
+    for m in range(1, 4):
+        put(ref["ds1"].at[(z ^ m) % 4], ref["dz1"].at[m], st_dz1, front ^ (8 * m))
+    drains.append((st_dz1, 3, 3))
+    st_p = stage.take()
 
     @on_one
     def _():
@@ -633,48 +736,36 @@
             for m in range(1, 4):
                 total = total + ref["nz1"][m, i]
             ref["t1p"][i] = total
-
-    st_p = stage.take()
-
-    @on_one
-    def _():
-        arrived(st_z, 2)
-        for i in range(2):
-            total = ref["as3"][0, i] + ref["t1p"][i] + ref["az3"][1, i]
-            ref["pt3"][i] = total
-            ref["pk3"][2 * chip_y + i] = total
+        arrived(st, 28)
+        for i in range(2):
+            ref["as3"][1, i] = reduced(st, ref["a3"], ref["ar3"], 4, (1, i))
+            total = ref["t1p"][i] + reduced(st, ref["a3"], ref["ar3"], 4, (0, i))
+            ref["as3"][0, i] = total
+            ref["pk3"][0, 2 * chip_y + i] = total
+        for mask in (12, 13, 10, 11, 14, 15, 8, 9):
+            put(ref["as3"].at[1], ref["pk3"].at[1, pair], st_p, front ^ mask)
         for mask in (4, 5, 2, 3, 6, 7, 1):
-            put(ref["pt3"], ref["pk3"].at[pair], st_p, front ^ mask)
-
-    drains.append((st_p, 0, 14))
-    st_dz1 = stage.take()
-    arrived(st_d1, 28)
-    for w in range(4):
-        ref["ds1"][w] = dense_total(ref["sd1"], ref["dr1"], w)
-    for m in range(1, 4):
-        put(ref["ds1"].at[(z ^ m) % 4], ref["dz1"].at[m], st_dz1, front ^ (8 * m))
-    drains.append((st_dz1, 3, 3))
+            put(ref["as3"].at[0], ref["pk3"].at[0, pair], st_p, front ^ mask)
+
+    drains.append((st_p, 0, 30))
     st_dz2 = stage.take()
     arrived(st_d2, 14)
     for w in range(2):
         ref["ds2"][w] = dense_total(ref["sd2"], ref["dr2"], w)
     put(ref["ds2"].at[(z ^ 1) % 2], ref["dz2"].at[1], st_dz2, front ^ 8)
     drains.append((st_dz2, 1, 1))
-    arrived(st_dz0, 7)
-    total = ref["ds0"][z]
-    for m in range(1, 8):
-        total = total + ref["dz0"][m]
-    so_ref[:, 0, :] = total
-    arrived_by_core(st_p, 8, 6)
-
-    value2 = doubled(ref["fk"][3] - panel_backward(3, ref["pk3"]))
-    dense_backward(3, value2, ref["sd3"])
-    st_d3 = dense_send(ref["sd3"], ref["dr3"], 1)
     arrived(st_dz1, 3)
     total = ref["ds1"][z % 4]
     for m in range(1, 4):
         total = total + ref["dz1"][m]
     so_ref[:, 1, :] = total
+    arrived_by_core(st_p, 16, 14)
+
+    for u in range(SLOTS):
+        ref["pk3"][0, u] = ref["pk3"][0, u] + ref["pk3"][1, u]
+    value2 = doubled(ref["fk"][3] - panel_backward(3, ref["pk3"].at[0]))
+    dense_backward(3, value2, ref["sd3"])
+    st_d3 = dense_send(ref["sd3"], ref["dr3"], 1)
     arrived(st_dz2, 1)
     so_ref[:, 2, :] = ref["ds2"][z % 2] + ref["dz2"][1]
 
@@ -700,27 +791,26 @@
 
 
 def shards(right_side, inverse_top, inverse_second, inverse_third, inverse_fourth, panels, targets):
-    vmem = pl.BlockSpec(memory_space=pltpu.VMEM)
     anywhere = pl.BlockSpec(memory_space=pl.ANY)
-    smem = pl.BlockSpec(memory_space=pltpu.SMEM)
-    out = jax.ShapeDtypeStruct(right_side.shape, F32)
-    return pl.pallas_call(
+    results = pl.pallas_call(
         kernel,
-        out_shape=(out, out),
-        in_specs=[vmem, anywhere, anywhere, anywhere, anywhere, anywhere, smem],
-        out_specs=(vmem, vmem),
+        out_shape=pltpu.VMEM((2,) + right_side.shape, F32),
+        in_specs=[anywhere] * 7,
+        out_specs=pl.BlockSpec(memory_space=pltpu.VMEM),
         scratch_shapes=[pltpu.VMEM(shape, dtype) for shape, dtype in SCRATCH.values()]
         + [
             pltpu.SMEM((8, 8, 128), I32),
+            pltpu.SMEM((3, 1, 8), I32),
             pltpu.SemaphoreType.DMA((STAGE_COUNT,)),
             pltpu.SemaphoreType.DMA((STAGE_COUNT,)),
-            pltpu.SemaphoreType.DMA((8,)),
+            pltpu.SemaphoreType.DMA((12,)),
         ],
         compiler_params=pltpu.CompilerParams(
             collective_id=0, has_side_effects=True, vmem_limit_bytes=56 * 2**20
         ),
         name="tiers",
     )(right_side, inverse_top, inverse_second, inverse_third, inverse_fourth, panels, targets)
+    return results[0], results[1]
 
 
 def solution(mesh):

time: 83.3 us -> 75.8 us (0.910)
  Pallas kernels: 79.6 us -> 74.4 us
  local copies, waits for them, and re-layouts: 2.65 us -> 0.61 us
    pallas_call x1, Pallas kernels: 79.6 us -> 74.4 us  [shards(): pl.pallas_call(kernel, out_shape=pltpu.VMEM((2,) + right_side.shape, F32)...]
    unnamed x2 -> x0, local copies, waits for them, and re-layouts: 2.65 us -> none
where the time goes in v1:
time: 75.8 us; the launch traced here: 75.7 us
  Pallas kernels  74.4 us (98%)
    pallas_call x1, Pallas kernels, shards(): pl.pallas_call(kernel, out_shape=pltpu.VMEM((2,) + right_side.shape, F32)...  74.4 us

profile of v1, /device:TPU:1, one launch (start us, length us, event | category | flops | bytes accessed | tf_op | source)
XLA Modules:
  0.0 75.7 jit_solution(6186088948390189989)
XLA Ops:
  0.6 74.4 %tiers.1 = f32[2,8,4,128]{3,2,1,0:T(4,128)S(1)} custom-call(f32[8,4,128]{2,1,0:T(4,128)} %rs_hbm.1, f32[128,8192]{1,0:T(8,128)} %i0_ref.1, f32[128,4096]{1,0:T(8,128)} %i1_ref.1, f32[128,2048]{1,0:T(8,128)} %i2_ref.1, f32[128,1024]{1,0:T(8,128)} %i3_ref.1, f32[3,1024,128]{2,1,0:T(8,128)} %pn_ref.1, s32[3,1,8]{2,1,0:T(1,128)} %tg_hbm.1), custom_call_target="tpu_custom_call" | custom-call | tf_op jit(solution)/shard_map/tiers/pallas_call | solution.py:795
  75.1 0.6 slice_bitcast_fusion

commit v2 on v1

--- a/solution.py
+++ b/solution.py
@@ -51,7 +51,7 @@
         return self.count - 1
 
 
-STAGE_COUNT = 48
+STAGE_COUNT = 52
 
 SCRATCH = dict(
     v0=((128, 8192), F32), v1=((128, 4096), F32), v2=((128, 2048), F32), v3=((128, 1024), F32),
@@ -78,12 +78,14 @@
     t0p=((2, 2, 8, 128), F32), t1p=((2, 8, 128), F32),
     sd0=((2, 4, 8, 8, 128), F32), sd1=((2, 4, 4, 8, 128), F32), sd2=((2, 4, 2, 8, 128), F32), sd3=((2, 4, 1, 8, 128), F32),
     dx0=((4, 8, 8, 128), F32), dx1=((4, 4, 8, 128), F32), de0=((4, 8, 8, 128), F32), de1=((4, 4, 8, 128), F32),
-    dr0=((4, 8, 8, 128), F32), dr1=((4, 4, 8, 128), F32), dr2=((8, 2, 8, 128), F32), dr3=((8, 1, 8, 128), F32),
-    ds0=((8, 8, 128), F32), ds1=((4, 8, 128), F32), ds2=((2, 8, 128), F32),
-    dz0=((8, 8, 128), F32), dz1=((4, 8, 128), F32), dz2=((2, 8, 128), F32),
+    dr0=((4, 8, 8, 128), F32), dr1=((4, 4, 8, 128), F32), dr2=((16, 8, 128), F32), dr3=((8, 1, 8, 128), F32),
+    ds0=((8, 8, 128), F32), ds1=((4, 8, 128), F32),
+    dz0=((8, 8, 128), F32), dz1=((4, 8, 128), F32),
     fk=((4, 8, 128), F32),
+    gp=((2, 4, 256, 128), F32), gx=((2, 4, 256, 128), F32), gs=((4, 2, 256, 128), F32), gr=((4, 2, 256, 128), F32),
+    ga=((2, 4, 256, 128), F32), gc=((1024, 256), BF16),
     rs=((8, 4, 128), F32),
-    dummy=((168, 8, 128), F32),
+    dummy=((256, 8, 128), F32),
 )
 
 
@@ -93,6 +95,7 @@
     tgs, tg_ref, send_sem, recv_sem, load_sem = scratch[len(names) :]
     rs_ref, fo_ref, so_ref = ref["rs"], out_ref.at[0], out_ref.at[1]
     front = lax.axis_index("front")
+    side = lax.axis_index("rhs")
     core = front % 2
     chip_y = (front // 2) % 4
     d = front % 8
@@ -101,10 +104,10 @@
     stage = Stage()
     drains = []
 
-    def put(src, dst, st, to):
+    def put(src, dst, st, to, axis="front"):
         pltpu.make_async_remote_copy(
             src_ref=src, dst_ref=dst, send_sem=send_sem.at[st], recv_sem=recv_sem.at[st],
-            device_id={"front": to}, device_id_type=MESH,
+            device_id={axis: to}, device_id_type=MESH,
         ).start()
 
     def drain(sem, blocks):
@@ -127,6 +130,8 @@
     masks = list(range(1, 16)) + [8 * m for m in range(2, 8)]
     for mask in masks:
         pl.semaphore_signal(barrier, inc=1, device_id={"front": front ^ mask}, device_id_type=MESH)
+    for k in range(1, 4):
+        pl.semaphore_signal(barrier, inc=1, device_id={"rhs": side ^ k}, device_id_type=MESH)
 
     loads = {}
     rs_copy = pltpu.make_async_copy(rs_hbm, rs_ref, load_sem.at[8])
@@ -154,7 +159,7 @@
             own_targets = jnp.where(lanes == k * 8 + u, tg_ref[k, 0, u], own_targets)
     ref["tgv"][z] = own_targets
 
-    pl.semaphore_wait(barrier, len(masks))
+    pl.semaphore_wait(barrier, len(masks) + 3)
 
     st_r3 = stage.take()
     for mask in (4, 5, 2, 3, 6, 7, 1):
@@ -285,10 +290,44 @@
     def on_one(body):
         pl.when(is_one)(body)
 
+    def on_zero(body):
+        pl.when(jnp.logical_not(is_one))(body)
+
     pair = pl.ds(2 * chip_y, 2)
+
+    def dense_send(out, into, blocks):
+        st_d = stage.take()
+        for mask in (4, 5, 2, 3, 6, 7, 1):
+            put(out.at[core ^ (mask & 1), chip_y ^ (mask >> 1)], into.at[mask], st_d, front ^ mask)
+        drains.append((st_d, 7 * blocks, 7 * blocks))
+        return st_d
+
+    def dense_total(out, into, index):
+        total = out[core, chip_y, index]
+        for mask in range(1, 8):
+            total = total + into[mask, index]
+        return total
+
+
+    st_rp = [None] * 3
+    st_rc = [None] * 3
+
+    def plane_gather(t):
+        st_rp[t] = stage.take()
+        for mask in (4, 2, 6):
+            put(rb[t].at[:, core, chip_y], rb[t].at[:, core, chip_y], st_rp[t], front ^ mask)
+        drains.append((st_rp[t], 3 * PLANES[t], 3 * PLANES[t]))
+
+    def core_gather(t):
+        arrived(st_rp[t], 3 * PLANES[t])
+        st_rc[t] = stage.take()
+        put(rb[t].at[:, core], rb[t].at[:, core], st_rc[t], front ^ 1)
+        drains.append((st_rc[t], 4 * PLANES[t], 4 * PLANES[t]))
 
     prepare_inverse(3)
     prepare_panel(3)
+    arrived(st_rz[2], 1)
+    plane_gather(2)
     arrived(st_r3, 7)
     forward3 = dense_forward(3)
     panel_forward(3, forward3, ref["up3"])
@@ -298,25 +337,11 @@
     arrived(st_tg, 7)
     targets_copy = pltpu.make_async_copy(ref["tgv"], tgs, load_sem.at[7])
     targets_copy.start()
-    arrived(st_rz[2], 1)
-    st_rp = [None] * 3
-    st_rc = [None] * 3
-
-    def plane_gather(t):
-        st_rp[t] = stage.take()
-        for mask in (4, 2, 6):
-            put(rb[t].at[:, core, chip_y], rb[t].at[:, core, chip_y], st_rp[t], front ^ mask)
-        drains.append((st_rp[t], 3 * PLANES[t], 3 * PLANES[t]))
-
-    def core_gather(t):
-        arrived(st_rp[t], 3 * PLANES[t])
-        st_rc[t] = stage.take()
-        put(rb[t].at[:, core], rb[t].at[:, core], st_rc[t], front ^ 1)
-        drains.append((st_rc[t], 4 * PLANES[t], 4 * PLANES[t]))
-
-    plane_gather(2)
+    dense_backward(3, doubled(forward3), ref["sd3"])
+    st_d3 = dense_send(ref["sd3"], ref["dr3"], 1)
     prepare_inverse(2)
     targets_copy.wait()
+    core_gather(2)
     st_s3 = stage.take()
     st_z3 = stage.take()
 
@@ -336,10 +361,24 @@
 
     drains.append((st_s3, 0, 30))
     drains.append((st_z3, 0, 12))
-    core_gather(2)
+    arrived(st_rz[1], 3)
+    plane_gather(1)
     prepare_panel(2)
     arrived(st_rc[2], 8)
     base2 = dense_forward(2)
+    quarter = pl.ds(pl.multiple_of(side * 256, 256), 256)
+    panel_rows = ref["pc"][2, quarter, :]
+    swapped = jnp.concatenate([panel_rows[:, 128:], panel_rows[:, :128]], axis=1)
+    for j in range(8):
+        product = matmul(panel_rows, cc[3][j], NATURAL) + matmul(swapped, cc[3][j], NATURAL)
+        ref["gp"][j % 2, j // 2] = product
+    st_gx = stage.take()
+
+    @on_one
+    def _():
+        put(ref["gp"], ref["gx"], st_gx, front ^ 1)
+
+    drains.append((st_gx, 0, 256))
     arrived_by_core(st_s3, 16, 14)
 
     forward2 = base2
@@ -349,9 +388,9 @@
     st = reduce_send(ref["up2"], ref["ur2"], 2)
     fo_ref[:, 2, :] = forward2
     ref["fk"][2] = forward2
-    arrived(st_rz[1], 3)
-    plane_gather(1)
-    prepare_inverse(1)
+    core_gather(1)
+    arrived(st_rz[0], 7)
+    plane_gather(0)
     st_q3 = stage.take()
 
     @on_one
@@ -365,6 +404,29 @@
             put(ref["uz3"].at[pl.ds(2, 2)], ref["s3q"].at[:, pair], st_q3, front ^ mask)
 
     drains.append((st_q3, 0, 12))
+    st_gr = [stage.take(), stage.take()]
+
+    def combined_send(half):
+        rows = pl.ds(128 * half, 128)
+        for k in (2, 1, 3):
+            put(ref["gs"].at[chip_y ^ k, :, rows], ref["gr"].at[k, :, rows], st_gr[half], front ^ (2 * k))
+
+    drains.append((st_gr[0], 96, 0))
+    drains.append((st_gr[1], 96, 0))
+
+    @on_zero
+    def _():
+        arrived(st_gx, 256)
+
+        def add_cross(y, carry):
+            for c in range(2):
+                ref["gs"][y, c] = ref["gp"][c, y] + ref["gx"][c, y]
+            return carry
+
+        lax.fori_loop(0, 4, add_cross, 0)
+        combined_send(0)
+
+    prepare_inverse(1)
     st_z2 = stage.take()
     st_z2b = stage.take()
 
@@ -380,7 +442,6 @@
 
     drains.append((st_z2, 0, 6))
     drains.append((st_z2b, 0, 8))
-    core_gather(1)
     st_q3c = stage.take()
 
     @on_one
@@ -408,7 +469,9 @@
 
     drains.append((st_s2, 0, 28))
 
-    @pl.when(jnp.logical_not(is_one))
+    core_gather(0)
+
+    @on_zero
     def _():
         arrived(st_q3c, 16)
 
@@ -442,8 +505,13 @@
 
     drains.append((st_q2, 0, 28))
     drains.append((st_r3x, 0, 24))
-    arrived(st_rz[0], 7)
-    plane_gather(0)
+
+    @on_zero
+    def _():
+        combined_send(1)
+
+    arrived(st_d3, 7)
+    solved3 = dense_total(ref["sd3"], ref["dr3"], 0)
     prepare_inverse(0)
     st_z1 = stage.take()
 
@@ -456,7 +524,6 @@
             put(ref["us1"], ref["uz1"].at[m], st_z1, front ^ (8 * m))
 
     drains.append((st_z1, 0, 14))
-    core_gather(0)
     st_r3c = stage.take()
 
     @on_one
@@ -530,19 +597,6 @@
 
     drains.append((st_nx, 96, 0))
 
-    def dense_send(out, into, blocks):
-        st_d = stage.take()
-        for mask in (4, 5, 2, 3, 6, 7, 1):
-            put(out.at[core ^ (mask & 1), chip_y ^ (mask >> 1)], into.at[mask], st_d, front ^ mask)
-        drains.append((st_d, 7 * blocks, 7 * blocks))
-        return st_d
-
-    def dense_total(out, into, index):
-        total = out[core, chip_y, index]
-        for mask in range(1, 8):
-            total = total + into[mask, index]
-        return total
-
     def chip_send(out, into, blocks):
         st_x = stage.take()
         put(out.at[1 - core], into, st_x, front ^ 1)
@@ -582,6 +636,18 @@
             put(ref["as1"].at[m >> 2], ref["az1"].at[m], st_z, front ^ (8 * m))
 
     drains.append((st_z, 0, 14))
+    st_ga = stage.take()
+
+    @on_zero
+    def _():
+        arrived(st_gr[0], 96)
+        arrived(st_gr[1], 96)
+        for c in range(2):
+            ref["ga"][c, side] = (ref["gs"][chip_y, c] + ref["gr"][1, c]) + (ref["gr"][2, c] + ref["gr"][3, c])
+        for k in (2, 1, 3):
+            put(ref["ga"].at[:, side], ref["ga"].at[:, side], st_ga, side ^ k, "rhs")
+
+    drains.append((st_ga, 192, 0))
     st_n0 = stage.take()
 
     @on_one
@@ -654,6 +720,14 @@
             ref["n1"][u // 2, m, u % 2] = ref["sd1"][tag & 1, (tag >> 1) & 3, (tag >> 3) & 3] * live
     st_n1 = reduce_send(ref["n1"], ref["nr1"], 8)
     st_dx1 = chip_send(ref["sd1"], ref["dx1"], 4)
+    st_gd = stage.take()
+
+    @on_zero
+    def _():
+        arrived(st_ga, 192)
+        put(ref["ga"].at[1], ref["ga"].at[1], st_gd, front ^ 1)
+
+    drains.append((st_gd, 128, 0))
 
     st_z = stage.take()
 
@@ -719,7 +793,13 @@
         slots_backward(2, 2, h, value2, ref["a3"], h)
     st = reduce_send(ref["a3"], ref["ar3"], 4)
     dense_backward(2, value2, ref["sd2"])
-    st_d2 = dense_send(ref["sd2"], ref["dr2"], 2)
+    st_d2 = stage.take()
+    for mask in (12, 13, 14, 15, 10, 11, 8, 9, 4, 5, 6, 7, 2, 3, 1):
+        put(
+            ref["sd2"].at[core ^ (mask & 1), chip_y ^ ((mask >> 1) & 3), (z ^ (mask >> 3)) % 2],
+            ref["dr2"].at[mask], st_d2, front ^ mask,
+        )
+    drains.append((st_d2, 15, 15))
 
     st_dz1 = stage.take()
     plane_total(st_d1, ref["de1"], ref["dr1"], ref["ds1"], 4)
@@ -748,12 +828,25 @@
             put(ref["as3"].at[0], ref["pk3"].at[0, pair], st_p, front ^ mask)
 
     drains.append((st_p, 0, 30))
-    st_dz2 = stage.take()
-    arrived(st_d2, 14)
-    for w in range(2):
-        ref["ds2"][w] = dense_total(ref["sd2"], ref["dr2"], w)
-    put(ref["ds2"].at[(z ^ 1) % 2], ref["dz2"].at[1], st_dz2, front ^ 8)
-    drains.append((st_dz2, 1, 1))
+
+    @on_one
+    def _():
+        arrived(st_gd, 128)
+
+    def split_combined(x, carry):
+        block = ref["ga"][core, x]
+        high = block.astype(BF16)
+        rows = pl.ds(pl.multiple_of(x * 256, 256), 256)
+        ref["gc"][rows, 0:128] = high
+        ref["gc"][rows, 128:256] = (block - high.astype(F32)).astype(BF16)
+        return carry
+
+    lax.fori_loop(0, 4, split_combined, 0)
+    arrived(st_d2, 15)
+    total = ref["sd2"][core, chip_y, z % 2]
+    for mask in range(1, 16):
+        total = total + ref["dr2"][mask]
+    so_ref[:, 2, :] = total
     arrived(st_dz1, 3)
     total = ref["ds1"][z % 4]
     for m in range(1, 4):
@@ -763,30 +856,25 @@
 
     for u in range(SLOTS):
         ref["pk3"][0, u] = ref["pk3"][0, u] + ref["pk3"][1, u]
-    value2 = doubled(ref["fk"][3] - panel_backward(3, ref["pk3"].at[0]))
-    dense_backward(3, value2, ref["sd3"])
-    st_d3 = dense_send(ref["sd3"], ref["dr3"], 1)
-    arrived(st_dz2, 1)
-    so_ref[:, 2, :] = ref["ds2"][z % 2] + ref["dz2"][1]
+    x = jnp.concatenate([ref["pk3"][0, u] for u in range(SLOTS)], axis=1)
+    so_ref[:, 3, :] = solved3 - fold_all(matmul(split_rows(x), ref["gc"][...], NATURAL))
 
     @on_one
     def _():
         for st_x, _zero, one in drains:
             left = one
             while left:
-                drain(send_sem.at[st_x], min(left, 168))
-                left -= min(left, 168)
+                drain(send_sem.at[st_x], min(left, 256))
+                left -= min(left, 256)
 
     @pl.when(jnp.logical_not(is_one))
     def _():
         for st_x, zero, _one in drains:
             left = zero
             while left:
-                drain(send_sem.at[st_x], min(left, 168))
-                left -= min(left, 168)
-
-    arrived(st_d3, 7)
-    so_ref[:, 3, :] = dense_total(ref["sd3"], ref["dr3"], 0)
+                drain(send_sem.at[st_x], min(left, 256))
+                left -= min(left, 256)
+
     assert stage.count <= STAGE_COUNT
 
 

time: 75.8 us -> 73.3 us (0.967)
  Pallas kernels: 74.4 us -> 71.9 us
    pallas_call x1, Pallas kernels: 74.4 us -> 71.9 us  [shards(): pl.pallas_call(kernel, out_shape=pltpu.VMEM((2,) + right_side.shape, F32)...]
where the time goes in v2:
time: 73.3 us; the launch traced here: 73.1 us
  Pallas kernels  71.9 us (98%)
    pallas_call x1, Pallas kernels, shards(): pl.pallas_call(kernel, out_shape=pltpu.VMEM((2,) + right_side.shape, F32)...  71.9 us

profile of v2, /device:TPU:1, one launch (start us, length us, event | category | flops | bytes accessed | tf_op | source)
XLA Modules:
  0.0 73.1 jit_solution(8089379904649382633)
XLA Ops:
  0.6 71.9 %tiers.1 = f32[2,8,4,128]{3,2,1,0:T(4,128)S(1)} custom-call(f32[8,4,128]{2,1,0:T(4,128)} %rs_hbm.1, f32[128,8192]{1,0:T(8,128)} %i0_ref.1, f32[128,4096]{1,0:T(8,128)} %i1_ref.1, f32[128,2048]{1,0:T(8,128)} %i2_ref.1, f32[128,1024]{1,0:T(8,128)} %i3_ref.1, f32[3,1024,128]{2,1,0:T(8,128)} %pn_ref.1, s32[3,1,8]{2,1,0:T(1,128)} %tg_hbm.1), custom_call_target="tpu_custom_call" | custom-call | tf_op jit(solution)/shard_map/tiers/pallas_call | solution.py:883
  72.5 0.6 slice_bitcast_fusion
